TPU v7x, 32 devices: a whole 2x2x4 slice. The times are simulated.
32 devices in a mesh: band: 4 (over y, core), tile: 8 (over z, x).
Axes of the slice: x: 2, y: 2, z: 4, core: 2. Of those that a mesh axis runs over, the one named last changes fastest.
Arguments:
- ocean_state: float32 [6, 64, 64, 1024], P(None, None, 'band', 'tile'), may hold values from -6 to 6
- forcing: float32 [6, 64, 64, 1024], P(None, None, 'band', 'tile')
- diffusivity: float32 [64, 1024], P('band', 'tile'), may hold values from 0.05 to 0.4
- land_sea: int32 [64, 1024], P('band', 'tile'), may hold values 0 or 1
- aggregate: int32 [64, 1024], P('band', 'tile'), may hold values from 0 to 63, as said below
- mixing: float32 [6, 6], replicated, may hold values from -2.5 to 2.5
- null_fields: float32 [2, 64, 2048], P(None, None, ('band', 'tile'))
- coarse_op: float32 [2048, 256], P('tile'), as said below
Outputs:
- new_state: float32 [6, 64, 64, 1024], P(None, None, 'band', 'tile')
- residual: float32 [6, 64, 64, 1024], P(None, None, 'band', 'tile')
Inputs may be any that keep to these rules, and one draw needn't show every extreme that they name: `aggregate`: each coarse block of a device takes exactly 32 of that device's cells. `coarse_op`: each block of 256 rows has a positive diagonal.
All inputs are finite; a program needn't handle non-finite values. No bound on the sum of `land_sea` on one device may be relied on, other than what follows from the above.
Results may differ from a plain program's by a relative error of at most 0.0001.
Values sent between devices are 32-bit elements; how exact they have to be, the bound alone decides.
A program may use at most 192 MiB of HBM per device.

v0:
```python
import jax
import jax.numpy as jnp
from jax import lax
from jax.sharding import PartitionSpec as P

SWEEPS = 3


SPEED_TABLE = (0.3, -0.2, 0.1, 0.25, -0.15, 0.05)
VERTICAL_MIX = 0.3
TIME_WEIGHT = 0.5
RESTRICT_SCALE = 0.25


def padded_2(block, sides, width):
    for axis, dim in sides:
        count = lax.axis_size(axis)
        forward = [(i, i + 1) for i in range(count - 1)]
        backward = [(target, source) for source, target in forward]
        low = lax.ppermute(
            lax.slice_in_dim(block, block.shape[dim] - width, None, axis=dim), axis, forward
        )
        high = lax.ppermute(lax.slice_in_dim(block, 0, width, axis=dim), axis, backward)
        block = jnp.concatenate([low, block, high], axis=dim)
    return block


def stencil(padded, diffusivity, ocean_mask, mixing):
    center = padded[:, :, 1:-1, 1:-1]
    laplace_h = (
        padded[:, :, 2:, 1:-1]
        + padded[:, :, :-2, 1:-1]
        + padded[:, :, 1:-1, 2:]
        + padded[:, :, 1:-1, :-2]
        - 4.0 * center
    )
    zonal_diff = padded[:, :, 1:-1, 2:] - padded[:, :, 1:-1, :-2]
    column_pad = jnp.pad(center, ((0, 0), (1, 1), (0, 0), (0, 0)))
    laplace_z = column_pad[:, 2:] + column_pad[:, :-2] - 2.0 * center
    coupled = jnp.einsum("fg,gzyx->fzyx", mixing, center, precision=lax.Precision.HIGHEST)
    speeds = jnp.array(SPEED_TABLE, dtype=jnp.float32)[:, None, None, None]
    inner = (
        center - diffusivity * laplace_h - VERTICAL_MIX * laplace_z + speeds * zonal_diff + coupled
    )
    return ocean_mask * inner + (1.0 - ocean_mask) * center


def moments(null_pair, coarse):
    gram = jnp.einsum("kzc,lzc->klz", null_pair, null_pair, precision=lax.Precision.HIGHEST)
    proj = jnp.einsum("kzc,fzc->kfz", null_pair, coarse, precision=lax.Precision.HIGHEST)
    return (gram, proj)


def shards(ocean_state, forcing, diffusivity, land_sea, aggregate, mixing, null_fields, coarse_op):
    ocean_mask = land_sea.astype(jnp.float32)

    def apply_once(field):
        padded = padded_2(field, (("band", 2), ("tile", 3)), 1)
        return stencil(padded, diffusivity, ocean_mask, mixing)

    first_jvp = apply_once(ocean_state)
    second_jvp = apply_once(first_jvp)
    residual = forcing - (first_jvp + TIME_WEIGHT * second_jvp)
    fields_count, depth_count, lat_cells, lon_cells = residual.shape
    blocks_dev = null_fields.shape[2]
    one_hot = (
        aggregate.reshape(-1)[:, None] == jnp.arange(blocks_dev, dtype=jnp.int32)[None, :]
    ).astype(jnp.float32)
    flat_rows = residual.reshape(fields_count * depth_count, lat_cells * lon_cells)
    coarse = jnp.dot(flat_rows, one_hot, precision=lax.Precision.HIGHEST)
    coarse = RESTRICT_SCALE * coarse.reshape(fields_count, depth_count, blocks_dev)
    gram_part, proj_part = moments(null_fields, coarse)
    gram, proj = lax.psum((gram_part, proj_part), "tile")
    determinant = gram[0, 0] * gram[1, 1] - gram[0, 1] * gram[0, 1]
    coef_first = (gram[1, 1] * proj[0] - gram[0, 1] * proj[1]) / determinant
    coef_second = (gram[0, 0] * proj[1] - gram[0, 1] * proj[0]) / determinant
    deflated = (
        coarse
        - coef_first[..., None] * null_fields[0][None]
        - coef_second[..., None] * null_fields[1][None]
    )
    diagonal_vals = jnp.diagonal(coarse_op)[None, :]
    coarse_block = lax.all_to_all(deflated, "band", split_axis=1, concat_axis=2, tiled=True)
    column_rows = coarse_block.reshape(-1, coarse_block.shape[2])
    iterate = jnp.zeros_like(column_rows)
    for sweep_index in range(SWEEPS):
        applied = jnp.einsum("rc,jc->rj", iterate, coarse_op, precision=lax.Precision.HIGHEST)
        iterate = iterate + (column_rows - applied) / diagonal_vals
    columns_done = iterate.reshape(coarse_block.shape)
    smoothed = lax.all_to_all(columns_done, "band", split_axis=2, concat_axis=1, tiled=True)
    correction = lax.dot_general(
        smoothed.reshape(fields_count * depth_count, blocks_dev),
        one_hot,
        (((1,), (1,)), ((), ())),
        precision=lax.Precision.HIGHEST,
    )
    new_state = ocean_state + correction.reshape(fields_count, depth_count, lat_cells, lon_cells)
    return (new_state, residual)


def solution(mesh):
    return jax.shard_map(
        shards,
        mesh=mesh,
        in_specs=(
            P(None, None, "band", "tile"),
            P(None, None, "band", "tile"),
            P("band", "tile"),
            P("band", "tile"),
            P("band", "tile"),
            P(),
            P(None, None, ("band", "tile")),
            P("tile", None),
        ),
        out_specs=(P(None, None, "band", "tile"), P(None, None, "band", "tile")),
        check_vma=False,
    )
```

profile of v0, /device:TPU:0, one launch (start us, length us, event | category | flops | bytes accessed | tf_op | source)
XLA Modules:
  0.0 220.4 jit_solution(14582239310134187766)
XLA Ops:
  0.7 3.9 %copy.106 = f32[6,64,16,128]{3,0,2,1:T(8,128)S(1)} copy(f32[6,64,16,128]{3,2,1,0:T(8,128)} %param.10) | data formatting | bytes 6291456 | tf_op args[0]
  4.6 2.4 %collective-permute-start.1 = (f32[6,64,1,128]{3,0,2,1:T(8,128)S(1)}, f32[6,64,1,128]{3,0,2,1:T(8,128)S(1)}, u32[]{:S(2)}, u32[]{:S(2)}) collective-permute-start(f32[6,64,1,128]{3,0,2,1:T(8,128)S(1)} %get-tuple-element.22), channel_id=1, source_target_pairs={{0,8},{8,16},{16,24},{1,9},{9,17},{17,25},{2,10},{10,18},{18,26},{... | collective-permute-start | bytes 589832 | tf_op jit(solution)/shard_map/ppermute | solution.py:20
  9.1 1.9 copy_dynamic-update-slice_fusion
  13.3 5.1 %fusion.45 = (f32[6,64,18,1]{3,0,2,1:T(8,128)}, f32[6,64,18,1]{3,0,2,1:T(8,128)}) fusion(f32[6,64,18,128]{3,0,2,1:T(8,128)S(1)} %constant_dynamic-update-slice_fusion), kind=kLoop, calls=%fused_computation.82 | loop fusion | bytes 110592 | tf_op jit(solution)/shard_map/slice | solution.py:21
  18.5 3.0 %copy.101 = f32[6,64,18,1]{1,3,2,0:T(1,128)S(1)} copy(f32[6,64,18,1]{3,0,2,1:T(8,128)} %get-tuple-element.18) | data formatting | bytes 55296 | tf_op jit(solution)/shard_map/slice | solution.py:23
  22.7 3.6 %copy.103 = f32[6,64,18,1]{1,3,2,0:T(1,128)} copy(f32[6,64,18,1]{3,0,2,1:T(8,128)} %get-tuple-element.17) | data formatting | bytes 55296 | tf_op jit(solution)/shard_map/slice | solution.py:21
  26.4 5.2 %collective-permute-start.3 = (f32[6,64,18,1]{1,3,2,0:T(1,128)}, f32[6,64,18,1]{1,3,2,0:T(1,128)}, u32[]{:S(2)}, u32[]{:S(2)}) collective-permute-start(f32[6,64,18,1]{1,3,2,0:T(1,128)} %copy.103), channel_id=1, source_target_pairs={{0,1},{1,2},{2,3},{3,4},{4,5},{5,6},{6,7},{8,9},{9,10},{10,11},{11... | collective-permute-start | bytes 82952 | tf_op jit(solution)/shard_map/ppermute | solution.py:20
  31.6 3.0 %copy.102 = f32[6,64,18,1]{3,0,2,1:T(8,128)} copy(f32[6,64,18,1]{1,3,2,0:T(1,128)S(1)} %collective-permute-done.2) | data formatting | bytes 55296 | tf_op jit(solution)/shard_map/ppermute | solution.py:23
  34.6 3.7 %copy.104 = f32[6,64,18,1]{3,0,2,1:T(8,128)} copy(f32[6,64,18,1]{1,3,2,0:T(1,128)} %collective-permute-done.3) | data formatting | bytes 55296 | tf_op jit(solution)/shard_map/ppermute | solution.py:20
  38.3 17.7 %fusion.24 = f32[6,64,16,128]{3,0,2,1:T(8,128)S(1)} fusion(f32[6,64,16,128]{3,0,2,1:T(8,128)} %copy-done.3, f32[6,64,1,128]{3,0,2,1:T(8,128)} %copy-done.9, f32[6,64,1,128]{3,0,2,1:T(8,128)} %copy-done.10, f32[6,64,18,1]{3,0,2,1:T(8,128)} %copy.102, f32[6,64,18,128]{3,0,2,1:T(8,128)} %copy-done.2, f32[6,64,18,1]{3,0,2,1:T(8,128)} %copy.104, ...), kind=kOutput, calls=%fused_computation.37 | convolution fusion | flops 74711040 | bytes 26239144 | tf_op jit(solution)/shard_map/fg,gzyx->fzyx/dot_general | solution.py:40
  57.6 6.8 %collective-permute-start.5 = (f32[6,64,1,128]{3,0,2,1:T(8,128)S(1)}, f32[6,64,1,128]{3,0,2,1:T(8,128)S(1)}, u32[]{:S(2)}, u32[]{:S(2)}) collective-permute-start(f32[6,64,1,128]{3,0,2,1:T(8,128)S(1)} %get-tuple-element.20), channel_id=1, source_target_pairs={{0,8},{8,16},{16,24},{1,9},{9,17},{17,25},{2,10},{10,18},{18,26},{... | collective-permute-start | bytes 589832 | tf_op jit(solution)/shard_map/ppermute | solution.py:20
  66.2 5.1 %fusion.44 = (f32[6,64,18,1]{3,0,2,1:T(8,128)}, f32[6,64,18,1]{3,0,2,1:T(8,128)}) fusion(f32[6,64,18,128]{3,0,2,1:T(8,128)S(1)} %pad_maximum_fusion), kind=kLoop, calls=%fused_computation.81 | loop fusion | bytes 110592 | tf_op jit(solution)/shard_map/slice | solution.py:21
  71.3 3.6 %copy.111 = f32[6,64,18,1]{1,3,2,0:T(1,128)} copy(f32[6,64,18,1]{3,0,2,1:T(8,128)} %get-tuple-element.16) | data formatting | bytes 55296 | tf_op jit(solution)/shard_map/slice | solution.py:23
  76.2 3.6 %copy.113 = f32[6,64,18,1]{1,3,2,0:T(1,128)} copy(f32[6,64,18,1]{3,0,2,1:T(8,128)} %get-tuple-element.15) | data formatting | bytes 55296 | tf_op jit(solution)/shard_map/slice | solution.py:21
  79.8 5.2 %collective-permute-start.7 = (f32[6,64,18,1]{1,3,2,0:T(1,128)}, f32[6,64,18,1]{1,3,2,0:T(1,128)}, u32[]{:S(2)}, u32[]{:S(2)}) collective-permute-start(f32[6,64,18,1]{1,3,2,0:T(1,128)} %copy.113), channel_id=1, source_target_pairs={{0,1},{1,2},{2,3},{3,4},{4,5},{5,6},{6,7},{8,9},{9,10},{10,11},{11... | collective-permute-start | bytes 82952 | tf_op jit(solution)/shard_map/ppermute | solution.py:20
  85.6 3.6 %copy.112 = f32[6,64,18,1]{3,0,2,1:T(8,128)} copy(f32[6,64,18,1]{1,3,2,0:T(1,128)} %collective-permute-done.6) | data formatting | bytes 55296 | tf_op jit(solution)/shard_map/ppermute | solution.py:23
  89.2 3.7 %copy.114 = f32[6,64,18,1]{3,0,2,1:T(8,128)} copy(f32[6,64,18,1]{1,3,2,0:T(1,128)} %collective-permute-done.7) | data formatting | bytes 55296 | tf_op jit(solution)/shard_map/ppermute | solution.py:20
  92.9 23.1 %fusion.13 = f32[6,64,16,128]{3,0,2,1:T(8,128)} fusion(f32[6,64,16,128]{3,0,2,1:T(8,128)} %copy-done.4, f32[6,64,1,128]{3,0,2,1:T(8,128)} %copy-done.8, f32[6,64,1,128]{3,0,2,1:T(8,128)} %copy-done.7, f32[6,64,16,128]{3,2,1,0:T(8,128)} %param.11, f32[6,64,18,1]{3,0,2,1:T(8,128)} %copy.112, f32[6,64,18,1]{3,0,2,1:T(8,128)} %copy.114, ...), kind=kOutput, calls=%fused_computation.22 | convolution fusion | flops 80216064 | bytes 24670720 | tf_op jit(solution)/shard_map/fg,gzyx->fzyx/dot_general | solution.py:40
  116.1 4.5 %copy.116 = f32[6,64,16,128]{3,2,1,0:T(8,128)} copy(f32[6,64,16,128]{3,0,2,1:T(8,128)} %fusion.13) | data formatting | bytes 6291456 | tf_op jit(solution)/shard_map/sub | solution.py:63
  120.5 4.5 %dot_general.36 = f32[6,64,2048]{2,1,0:T(8,128)} reshape(f32[6,64,16,128]{3,2,1,0:T(8,128)} %copy.116) | data formatting | bytes 6291456 | tf_op jit(solution)/shard_map/dot_general | solution.py:70
  125.1 3.4 %convolution_multiply_fusion = f32[6,64,64]{2,1,0:T(8,128)S(1)} fusion(f32[6,64,2048]{2,1,0:T(8,128)} %dot_general.36, s32[2048]{0:T(1024)S(1)} %bitcast.75), kind=kOutput, calls=%fused_computation.40 | convolution fusion | flops 604135424 | bytes 3252224 | tf_op jit(solution)/shard_map/dot_general | solution.py:70
  131.4 37.7 %all-reduce.2 = (f32[2,6,64]{2,1,0:T(8,128)}, f32[2,2,64]{0,1,2:T(2,128)S(1)}) all-reduce(f32[2,6,64]{2,1,0:T(8,128)S(1)} %bitcast.76, f32[2,2,64]{0,1,2:T(2,128)S(1)} %convolution_bitcast_fusion), channel_id=1, replica_groups=mesh['band'=4,'tile'=8] {'tile'}, use_global_device_ids=true, to_apply=%region_1.2 | all-reduce | flops 1024 | bytes 8192 | tf_op jit(solution)/shard_map/psum | solution.py:73
  174.6 8.0 %all-to-all-start = ((f32[4,1,6144]{2,1,0:T(1,128)}), f32[4,1,6144]{2,1,0:T(1,128)S(1)}, u32[]{:S(2)}, u32[]{:S(2)}) async-start(f32[4,1,6144]{2,1,0:T(1,128)} %reshape.181), calls=%async_computation | async-start | bytes 196608 | tf_op jit(solution)/shard_map/all_to_all | solution.py:83
  182.6 2.3 %gather_fusion = f32[256]{0:T(256)S(1)} fusion(f32[256,256]{1,0:T(8,128)S(1)} %copy-done, s32[256]{0:T(256)S(1)} %bitcast.67), kind=kCustom, calls=%fused_computation | custom fusion | bytes 4096 | tf_op jit(solution)/shard_map/jit(diagonal)/cond/branch_0_fun/gather | solution.py:82
  184.9 2.1 all-to-all-done
  195.6 2.2 copy.124
  197.8 2.2 %reshape.183 = f32[4,1,6144]{2,1,0:T(1,128)} reshape(f32[256,6,16]{2,1,0:T(8,128)} %bitcast.68) | data formatting | bytes 196608
  200.1 7.6 %all_to_all.30 = f32[4,1,6144]{2,1,0:T(1,128)S(1)} all-to-all(f32[4,1,6144]{2,1,0:T(1,128)} %reshape.183), channel_id=1, replica_groups=mesh['band'=4,'tile'=8] {'band'}, dimensions={0} | all-to-all | bytes 196608 | tf_op jit(solution)/shard_map/all_to_all | solution.py:90
  209.2 2.3 %reshape.184 = f32[256,6,16]{2,1,0:T(8,128)} reshape(f32[4,6144]{1,0:T(4,128)} %reduce.7) | data formatting | bytes 196608
  211.5 2.2 copy.125
  213.7 3.2 %copy_add_fusion = f32[6,64,16,128]{3,1,2,0:T(8,128)S(1)} fusion(f32[6,64,16,128]{3,2,1,0:T(8,128)S(1)} %copy-done.1, f32[6,64,64,1]{2,1,3,0:T(8,128)} %bitcast.72, s32[16,128]{1,0:T(8,128)S(1)} %copy-done.11), kind=kOutput, calls=%fused_computation.39 | convolution fusion | flops 604897280 | bytes 6397952 | tf_op jit(solution)/shard_map/dot_general | solution.py:91
  216.9 3.5 %copy.127 = f32[6,64,16,128]{3,2,1,0:T(8,128)} copy(f32[6,64,16,128]{3,1,2,0:T(8,128)S(1)} %copy_add_fusion) | data formatting | bytes 6291456
  (71 shorter events, 29.4 us)
Async XLA Ops:
  0.6 181.9 %copy-start = (f32[256,256]{1,0:T(8,128)S(1)}, f32[256,256]{1,0:T(8,128)}, u32[]{:S(2)}) copy-start(f32[256,256]{1,0:T(8,128)} %param.17) | copy-start | bytes 786436
  0.6 8.4 %copy-start.1 = (f32[6,64,16,128]{3,2,1,0:T(8,128)S(1)}, f32[6,64,16,128]{3,2,1,0:T(8,128)}, u32[]{:S(2)}) copy-start(f32[6,64,16,128]{3,2,1,0:T(8,128)} %param.10) | copy-start | bytes 9437188
  4.6 6.4 %copy-start.3 = (f32[6,64,16,128]{3,0,2,1:T(8,128)}, f32[6,64,16,128]{3,0,2,1:T(8,128)S(1)}, u32[]{:S(2)}) copy-start(f32[6,64,16,128]{3,0,2,1:T(8,128)S(1)} %copy.106) | copy-start | bytes 9437188
  4.6 3.7 %collective-permute-start.1 = (f32[6,64,1,128]{3,0,2,1:T(8,128)S(1)}, f32[6,64,1,128]{3,0,2,1:T(8,128)S(1)}, u32[]{:S(2)}, u32[]{:S(2)}) collective-permute-start(f32[6,64,1,128]{3,0,2,1:T(8,128)S(1)} %get-tuple-element.22), channel_id=1, source_target_pairs={{0,8},{8,16},{16,24},{1,9},{9,17},{17,25},{2,10},{10,18},{18,26},{... | collective-permute-start | bytes 589832 | tf_op jit(solution)/shard_map/ppermute | solution.py:20
  7.0 5.5 %collective-permute-start = (f32[6,64,1,128]{3,0,2,1:T(8,128)S(1)}, f32[6,64,1,128]{3,0,2,1:T(8,128)S(1)}, u32[]{:S(2)}, u32[]{:S(2)}) collective-permute-start(f32[6,64,1,128]{3,0,2,1:T(8,128)S(1)} %get-tuple-element.21), channel_id=1, source_target_pairs={{8,0},{16,8},{24,16},{9,1},{17,9},{25,17},{10,2},{18,10},{26,18},{... | collective-permute-start | bytes 589832 | tf_op jit(solution)/shard_map/ppermute | solution.py:23
  8.3 0.7 copy-start.9
  12.6 0.7 copy-start.10
  13.3 5.2 %copy-start.2 = (f32[6,64,18,128]{3,0,2,1:T(8,128)}, f32[6,64,18,128]{3,0,2,1:T(8,128)S(1)}, u32[]{:S(2)}) copy-start(f32[6,64,18,128]{3,0,2,1:T(8,128)S(1)} %constant_dynamic-update-slice_fusion) | copy-start | bytes 10616836
  18.5 13.1 %copy-start.12 = (s32[16,128]{1,0:T(8,128)S(1)}, s32[16,128]{1,0:T(8,128)}, u32[]{:S(2)}) copy-start(s32[16,128]{1,0:T(8,128)} %param.13) | copy-start | bytes 24580
  21.4 10.1 %collective-permute-start.2 = (f32[6,64,18,1]{1,3,2,0:T(1,128)S(1)}, f32[6,64,18,1]{1,3,2,0:T(1,128)S(1)}, u32[]{:S(2)}, u32[]{:S(2)}) collective-permute-start(f32[6,64,18,1]{1,3,2,0:T(1,128)S(1)} %copy.101), channel_id=1, source_target_pairs={{1,0},{2,1},{3,2},{4,3},{5,4},{6,5},{7,6},{9,8},{10,9},{11,10},{12... | collective-permute-start | bytes 82952 | tf_op jit(solution)/shard_map/ppermute | solution.py:23
  26.4 8.2 %collective-permute-start.3 = (f32[6,64,18,1]{1,3,2,0:T(1,128)}, f32[6,64,18,1]{1,3,2,0:T(1,128)}, u32[]{:S(2)}, u32[]{:S(2)}) collective-permute-start(f32[6,64,18,1]{1,3,2,0:T(1,128)} %copy.103), channel_id=1, source_target_pairs={{0,1},{1,2},{2,3},{3,4},{4,5},{5,6},{6,7},{8,9},{9,10},{10,11},{11... | collective-permute-start | bytes 82952 | tf_op jit(solution)/shard_map/ppermute | solution.py:20
  31.5 6.8 %copy-start.13 = (f32[16,128]{1,0:T(8,128)S(1)}, f32[16,128]{1,0:T(8,128)}, u32[]{:S(2)}) copy-start(f32[16,128]{1,0:T(8,128)} %param.12) | copy-start | bytes 24580
  31.5 6.8 %copy-start.14 = (f32[6,6]{1,0:T(8,128)S(1)}, f32[6,6]{1,0:T(8,128)}, u32[]{:S(2)}) copy-start(f32[6,6]{1,0:T(8,128)} %param.15) | copy-start | bytes 436
  31.5 6.8 %copy-start.15 = (f32[6]{0:T(128)S(1)}, f32[6]{0:T(128)}, u32[]{:S(2)}) copy-start(f32[6]{0:T(128)} %constant.23.clone) | copy-start | bytes 76
  38.3 26.0 %copy-start.6 = (f32[2,64,64]{2,1,0:T(8,128)S(1)}, f32[2,64,64]{2,1,0:T(8,128)}, u32[]{:S(2)}) copy-start(f32[2,64,64]{2,1,0:T(8,128)} %param.16) | copy-start | bytes 98308
  56.0 9.9 %copy-start.4 = (f32[6,64,16,128]{3,0,2,1:T(8,128)}, f32[6,64,16,128]{3,0,2,1:T(8,128)S(1)}, u32[]{:S(2)}) copy-start(f32[6,64,16,128]{3,0,2,1:T(8,128)S(1)} %fusion.24) | copy-start | bytes 9437188
  56.1 8.8 %collective-permute-start.4 = (f32[6,64,1,128]{3,0,2,1:T(8,128)S(1)}, f32[6,64,1,128]{3,0,2,1:T(8,128)S(1)}, u32[]{:S(2)}, u32[]{:S(2)}) collective-permute-start(f32[6,64,1,128]{3,0,2,1:T(8,128)S(1)} %get-tuple-element.19), channel_id=1, source_target_pairs={{8,0},{16,8},{24,16},{9,1},{17,9},{25,17},{10,2},{18,10},{26,18},{... | collective-permute-start | bytes 589832 | tf_op jit(solution)/shard_map/ppermute | solution.py:23
  57.6 7.9 %collective-permute-start.5 = (f32[6,64,1,128]{3,0,2,1:T(8,128)S(1)}, f32[6,64,1,128]{3,0,2,1:T(8,128)S(1)}, u32[]{:S(2)}, u32[]{:S(2)}) collective-permute-start(f32[6,64,1,128]{3,0,2,1:T(8,128)S(1)} %get-tuple-element.20), channel_id=1, source_target_pairs={{0,8},{8,16},{16,24},{1,9},{9,17},{17,25},{2,10},{10,18},{18,26},{... | collective-permute-start | bytes 589832 | tf_op jit(solution)/shard_map/ppermute | solution.py:20
  64.9 1.0 copy-start.7
  65.5 0.7 copy-start.8
  74.9 10.7 %collective-permute-start.6 = (f32[6,64,18,1]{1,3,2,0:T(1,128)}, f32[6,64,18,1]{1,3,2,0:T(1,128)}, u32[]{:S(2)}, u32[]{:S(2)}) collective-permute-start(f32[6,64,18,1]{1,3,2,0:T(1,128)} %copy.111), channel_id=1, source_target_pairs={{1,0},{2,1},{3,2},{4,3},{5,4},{6,5},{7,6},{9,8},{10,9},{11,10},{12... | collective-permute-start | bytes 82952 | tf_op jit(solution)/shard_map/ppermute | solution.py:23
  79.8 9.4 %collective-permute-start.7 = (f32[6,64,18,1]{1,3,2,0:T(1,128)}, f32[6,64,18,1]{1,3,2,0:T(1,128)}, u32[]{:S(2)}, u32[]{:S(2)}) collective-permute-start(f32[6,64,18,1]{1,3,2,0:T(1,128)} %copy.113), channel_id=1, source_target_pairs={{0,1},{1,2},{2,3},{3,4},{4,5},{5,6},{6,7},{8,9},{9,10},{10,11},{11... | collective-permute-start | bytes 82952 | tf_op jit(solution)/shard_map/ppermute | solution.py:20
  120.5 4.6 %copy-start.11 = (s32[16,128]{1,0:T(8,128)S(1)}, s32[16,128]{1,0:T(8,128)}, u32[]{:S(2)}) copy-start(s32[16,128]{1,0:T(8,128)} %param.14) | copy-start | bytes 24580
  128.5 0.7 copy-start.5
  174.6 12.5 %all-to-all-start = ((f32[4,1,6144]{2,1,0:T(1,128)}), f32[4,1,6144]{2,1,0:T(1,128)S(1)}, u32[]{:S(2)}, u32[]{:S(2)}) async-start(f32[4,1,6144]{2,1,0:T(1,128)} %reshape.181), calls=%async_computation | async-start | bytes 196608 | tf_op jit(solution)/shard_map/all_to_all | solution.py:83
where the time goes:
time: 222 us; the launch traced here: 220 us
  local copies, waits for them, and re-layouts  80.6 us (36%)
  matrix products  51.1 us (23%)
  blocking collectives  45.2 us (20%)
  starting transfers between devices  32.7 us (15%)
  other arithmetic  5.44 us (2%)
  waiting for transfers between devices  4.29 us (2%)
    dot_general x2, matrix products, stencil(): jnp.einsum('fg,gzyx->fzyx', mixing, center, precision=lax.Precision.HIGHEST)  40.8 us
    psum x1, blocking collectives, shards(): gram, proj = lax.psum((gram_part, proj_part), 'tile')  37.7 us
    unnamed x40, local copies, waits for them, and re-layouts  19.7 us
    ppermute x4, starting transfers between devices, padded_2(): lax.ppermute(lax.slice_in_dim(block, block.shape[dim] - width, None, axis...  19.4 us
    slice x4, local copies, waits for them, and re-layouts, padded_2(): lax.slice_in_dim(block, block.shape[dim] - width, None, axis=dim)  17.5 us
    all_to_all x1, starting transfers between devices, shards(): lax.all_to_all(deflated, 'band', split_axis=1, concat_axis=2, tiled=True)  7.96 us
    all_to_all x1, blocking collectives, shards(): lax.all_to_all(columns_done, 'band', split_axis=2, concat_axis=1, tiled=T...  7.57 us
    ppermute x2, local copies, waits for them, and re-layouts, padded_2(): lax.ppermute(lax.slice_in_dim(block, block.shape[dim] - width, None, axis...  7.43 us
  transfers between devices with their start and end apart: 9, of which 3 were waited for; matrix products, arithmetic and copies ran while one was open for 9% of the time, Pallas kernels for 0%

commit v1 on v0

v1 whole, which is shorter than its diff:
```python
import functools

import jax
import jax.numpy as jnp
from jax import lax
from jax.experimental import pallas as pl
from jax.experimental.pallas import tpu as pltpu
from jax.sharding import PartitionSpec as P

SWEEPS = 3
SPEED_TABLE = (0.3, -0.2, 0.1, 0.25, -0.15, 0.05)
VERTICAL_MIX = 0.3
TIME_WEIGHT = 0.5
RESTRICT_SCALE = 0.25

F32 = jnp.float32
BF16 = jnp.bfloat16
MESH = pl.DeviceIdType.MESH
PAD = 8
ZC = 16
MIB = 1 << 20


def nt_dot(a, b, precision=None):
    return lax.dot_general(
        a, b, (((1,), (1,)), ((), ())), precision=precision, preferred_element_type=F32
    )


def main_kernel(
    dims, ocean_ref, forcing_ref, diff_ref, land_ref, agg_ref, mix_ref, null_ref, op_ref,
    res_ref, smooth_ref,
    ocean, work, field0, field1, send_w, send_e, col_w, col_e, hi, lo, coarse,
    mom, slab_out, slab_in, back_out, back_in,
    in_sem, work_sem, out_sem, lat_send, lat_recv, lon_send, lon_recv,
    mom_send, mom_recv, slab_send, slab_recv, back_send, back_recv,
):
    n_band, n_tile, nf, nz, cy, cx, cb = dims
    band, tile = lax.axis_index("band"), lax.axis_index("tile")
    top = PAD + nz

    loads = [
        pltpu.make_async_copy(ocean_ref.at[f], ocean.at[f], in_sem.at[f]) for f in range(nf)
    ]
    for load in loads:
        load.start()
    load_forcing = pltpu.make_async_copy(forcing_ref, work, work_sem)
    load_forcing.start()

    barrier = pltpu.get_barrier_semaphore()
    for d in range(1, n_tile):
        pl.semaphore_signal(
            barrier, inc=1, device_id=(band, lax.rem(tile + d, n_tile)), device_id_type=MESH
        )
    for d in range(1, n_band):
        pl.semaphore_signal(
            barrier, inc=1, device_id=(lax.rem(band + d, n_band), tile), device_id_type=MESH
        )

    zpad = jnp.zeros((nf, cy + 2, PAD, cx), F32)
    for field in (field0, field1):
        field[:, :, 0:PAD, :] = zpad
        field[:, :, top : top + PAD, :] = zpad
    zrow = jnp.zeros((nf, nz, cx), F32)

    @pl.when(band == 0)
    def _():
        for field in (field0, field1):
            field[:, 0, PAD:top, :] = zrow

    @pl.when(band == n_band - 1)
    def _():
        for field in (field0, field1):
            field[:, cy + 1, PAD:top, :] = zrow

    zcol = jnp.zeros((2, nz, cx), F32)

    @pl.when(tile == 0)
    def _():
        col_w[...] = zcol

    @pl.when(tile == n_tile - 1)
    def _():
        col_e[...] = zcol

    send_w[...] = zcol
    send_e[...] = zcol
    coarse[...] = jnp.zeros_like(coarse)

    lane = lax.broadcasted_iota(jnp.int32, (ZC, cx), 1)

    def pack(which, value, rows, k):
        here = lane == k
        send_w[which, rows, :] = jnp.where(here, pltpu.roll(value, k, 1), send_w[which, rows, :])
        shift = lax.rem(k + 1, cx)
        send_e[which, rows, :] = jnp.where(
            here, pltpu.roll(value, shift, 1), send_e[which, rows, :]
        )

    for f in range(nf):
        loads[f].wait()

    def fill(y, carry):
        for f in range(nf):
            for z0 in range(0, nz, ZC):
                value = ocean[f, pl.ds(z0 * cy + y, ZC, stride=cy), :]
                field0[f, y + 1, PAD + z0 : PAD + z0 + ZC, :] = value
                pack(0, value, slice(z0, z0 + ZC), f * cy + y)
        return carry

    lax.fori_loop(0, cy, fill, 0)
    pl.semaphore_wait(barrier, n_tile + n_band - 2)

    def lat_copies(which, field):
        up = pltpu.make_async_remote_copy(
            src_ref=field.at[:, cy, PAD:top, :], dst_ref=field.at[:, 0, PAD:top, :],
            send_sem=lat_send.at[which, 0], recv_sem=lat_recv.at[which, 0],
            device_id=(band + 1, tile), device_id_type=MESH,
        )
        down = pltpu.make_async_remote_copy(
            src_ref=field.at[:, 1, PAD:top, :], dst_ref=field.at[:, cy + 1, PAD:top, :],
            send_sem=lat_send.at[which, 1], recv_sem=lat_recv.at[which, 1],
            device_id=(band - 1, tile), device_id_type=MESH,
        )
        return up, down

    def lon_copies(which):
        up = pltpu.make_async_remote_copy(
            src_ref=send_e.at[which], dst_ref=col_w.at[which],
            send_sem=lon_send.at[which, 0], recv_sem=lon_recv.at[which, 0],
            device_id=(band, tile + 1), device_id_type=MESH,
        )
        down = pltpu.make_async_remote_copy(
            src_ref=send_w.at[which], dst_ref=col_e.at[which],
            send_sem=lon_send.at[which, 1], recv_sem=lon_recv.at[which, 1],
            device_id=(band, tile - 1), device_id_type=MESH,
        )
        return up, down

    def start_both(copies, index, count):
        @pl.when(index < count - 1)
        def _():
            copies[0].start()

        @pl.when(index > 0)
        def _():
            copies[1].start()

    def recv_both(copies, index, count):
        @pl.when(index > 0)
        def _():
            copies[0].wait_recv()

        @pl.when(index < count - 1)
        def _():
            copies[1].wait_recv()

    def sent_both(copies, index, count):
        @pl.when(index < count - 1)
        def _():
            copies[0].wait_send()

        @pl.when(index > 0)
        def _():
            copies[1].wait_send()

    def exchange(which, field):
        lon, lat = lon_copies(which), lat_copies(which, field)
        start_both(lon, tile, n_tile)
        start_both(lat, band, n_band)
        return lon, lat

    def jacobian_rows(which, field, y, z0):
        at = PAD + z0
        rows = slice(at, at + ZC)
        center = [field[g, y + 1, rows, :] for g in range(nf)]
        diff = diff_ref[pl.ds(y, 1), :]
        main = 4.0 * diff + (1.0 + 2.0 * VERTICAL_MIX)
        ocean_cell = jnp.broadcast_to(land_ref[pl.ds(y, 1), :], (ZC, cx)) != 0
        west_in = col_w[which, z0 : z0 + ZC, :]
        east_in = col_e[which, z0 : z0 + ZC, :]
        outs = []
        for f in range(nf):
            c = center[f]
            k = f * cy + y
            west = jnp.where(lane == 0, pltpu.roll(west_in, cx - k, 1), pltpu.roll(c, 1, 1))
            east = jnp.where(
                lane == cx - 1, pltpu.roll(east_in, cx - 1 - k, 1), pltpu.roll(c, cx - 1, 1)
            )
            around = field[f, y, rows, :] + field[f, y + 2, rows, :] + (east + west)
            vert = field[f, y + 1, at - 1 : at - 1 + ZC, :] + field[f, y + 1, at + 1 : at + 1 + ZC, :]
            total = main * c - diff * around - VERTICAL_MIX * vert + SPEED_TABLE[f] * (east - west)
            for g in range(nf):
                total = total + mix_ref[f, g] * center[g]
            outs.append(jnp.where(ocean_cell, total, c))
        return center, outs

    def first(y, carry):
        for z0 in range(0, nz, ZC):
            center, outs = jacobian_rows(0, field0, y, z0)
            for f in range(nf):
                field1[f, y + 1, PAD + z0 : PAD + z0 + ZC, :] = outs[f]
                pack(1, outs[f], slice(z0, z0 + ZC), f * cy + y)
        return carry

    def second(y, carry):
        for z0 in range(0, nz, ZC):
            center, outs = jacobian_rows(1, field1, y, z0)
            for f in range(nf):
                spot = pl.ds(z0 * cy + y, ZC, stride=cy)
                value = work[f, spot, :] - (center[f] + TIME_WEIGHT * outs[f])
                work[f, spot, :] = value
                high = value.astype(BF16)
                hi[f * nz + z0 : f * nz + z0 + ZC, :] = high
                lo[f * nz + z0 : f * nz + z0 + ZC, :] = (value - high.astype(F32)).astype(BF16)
        block = lax.broadcasted_iota(jnp.int32, (cx, cx), 0)
        member = jnp.where(block == agg_ref[pl.ds(y, 1), :], 1.0, 0.0).astype(BF16)
        coarse[...] += nt_dot(hi[...], member) + nt_dot(lo[...], member)
        return carry

    ends = lambda body: lax.fori_loop(0, 2, lambda i, carry: body(i * (cy - 1), carry), 0)

    lon0, lat0 = exchange(0, field0)
    recv_both(lon0, tile, n_tile)
    lax.fori_loop(1, cy - 1, first, 0)
    recv_both(lat0, band, n_band)
    ends(first)
    lon1, lat1 = exchange(1, field1)
    load_forcing.wait()
    recv_both(lon1, tile, n_tile)
    lax.fori_loop(1, cy - 1, second, 0)
    recv_both(lat1, band, n_band)
    ends(second)
    store = pltpu.make_async_copy(work, res_ref, out_sem)
    store.start()

    nulls = [null_ref[0], null_ref[1]]
    parts = [RESTRICT_SCALE * coarse[f * nz : (f + 1) * nz, 0:cb] for f in range(nf)]
    products = [nulls[0] * nulls[0], nulls[0] * nulls[1], nulls[1] * nulls[1]]
    for k in range(2):
        products += [nulls[k] * part for part in parts]
    wide = lax.broadcasted_iota(jnp.int32, (nz, cx), 1)
    table = jnp.zeros((nz, cx), F32)
    for j, product in enumerate(products):
        table = jnp.where(wide == j, jnp.sum(product, axis=1, keepdims=True), table)
    square = jnp.concatenate([table, jnp.zeros((cx - nz, cx), F32)], axis=0)
    mom[tile] = jnp.transpose(square)[0:16, :]

    def mom_copy(partner, slot):
        return pltpu.make_async_remote_copy(
            src_ref=mom.at[tile], dst_ref=mom.at[slot],
            send_sem=mom_send.at[partner], recv_sem=mom_recv.at[slot],
            device_id=(band, partner), device_id_type=MESH,
        )

    for d in range(1, n_tile):
        mom_copy(lax.rem(tile + d, n_tile), tile).start()

    op = op_ref[...]
    ncol = op.shape[0]
    same = lax.broadcasted_iota(jnp.int32, (ncol, ncol), 0) == lax.broadcasted_iota(
        jnp.int32, (ncol, ncol), 1
    )
    diagonal = jnp.sum(jnp.where(same, op, 0.0), axis=0, keepdims=True)

    for d in range(1, n_tile):
        other = lax.rem(tile + d, n_tile)
        mom_copy(other, other).wait_recv()
    total = mom[0]
    for t in range(1, n_tile):
        total = total + mom[t]
    row = lambda j: total[j : j + 1, :]
    g00, g01, g11 = row(0), row(1), row(2)
    p0, p1 = total[3 : 3 + nf, :], total[3 + nf : 3 + 2 * nf, :]
    real = lax.broadcasted_iota(jnp.int32, (1, cx), 1) < nz
    det = jnp.where(real, g00 * g11 - g01 * g01, 1.0)
    c0 = (g11 * p0 - g01 * p1) / det
    c1 = (g00 * p1 - g01 * p0) / det
    coefs = jnp.concatenate([c0, c1, jnp.zeros((cx - 2 * nf, cx), F32)], axis=0)
    coefs = jnp.transpose(coefs)[0:nz, :]
    half = nf // 2
    deflated = [
        parts[f] - coefs[:, f : f + 1] * nulls[0] - coefs[:, nf + f : nf + f + 1] * nulls[1]
        for f in range(nf)
    ]
    slab = nz // n_band
    for f in range(half):
        both = jnp.concatenate([deflated[f], deflated[f + half]], axis=1)
        for d in range(n_band):
            slab_out[d, f * slab : (f + 1) * slab, :] = both[d * slab : (d + 1) * slab, :]

    def band_copy(out, into, sends, recvs, partner, slot):
        return pltpu.make_async_remote_copy(
            src_ref=out.at[partner], dst_ref=into.at[slot],
            send_sem=sends.at[partner], recv_sem=recvs.at[slot],
            device_id=(partner, tile), device_id_type=MESH,
        )

    def swap(out, into, sends, recvs):
        for d in range(1, n_band):
            band_copy(out, into, sends, recvs, lax.rem(band + d, n_band), band).start()
        into[band] = out[band]
        for d in range(1, n_band):
            other = lax.rem(band + d, n_band)
            band_copy(out, into, sends, recvs, other, other).wait_recv()

    swap(slab_out, slab_in, slab_send, slab_recv)
    pieces = [slab_in[b] for b in range(n_band)]
    lows = jnp.concatenate([piece[:, 0:cb] for piece in pieces], axis=1)
    highs = jnp.concatenate([piece[:, cb : 2 * cb] for piece in pieces], axis=1)
    columns = jnp.concatenate([lows, highs], axis=0)
    iterate = columns / diagonal
    for _ in range(SWEEPS - 1):
        applied = nt_dot(iterate, op, lax.Precision.HIGHEST)
        iterate = iterate + (columns - applied) / diagonal
    rows_half = half * slab
    for b in range(n_band):
        mine = slice(b * cb, (b + 1) * cb)
        back_out[b] = jnp.concatenate(
            [iterate[0:rows_half, mine], iterate[rows_half : 2 * rows_half, mine]], axis=1
        )
    swap(back_out, back_in, back_send, back_recv)
    inside = lax.broadcasted_iota(jnp.int32, (slab, 2 * cb), 1) < cb
    for d in range(n_band):
        for f in range(half):
            both = back_in[d, f * slab : (f + 1) * slab, :]
            z = slice(d * slab, (d + 1) * slab)
            smooth_ref[f, z, :] = jnp.where(inside, both, 0.0)
            smooth_ref[f + half, z, :] = jnp.where(inside, pltpu.roll(both, cb, 1), 0.0)

    for lon, lat in ((lon0, lat0), (lon1, lat1)):
        sent_both(lon, tile, n_tile)
        sent_both(lat, band, n_band)
    for d in range(1, n_tile):
        mom_copy(lax.rem(tile + d, n_tile), tile).wait_send()
    for d in range(1, n_band):
        other = lax.rem(band + d, n_band)
        band_copy(slab_out, slab_in, slab_send, slab_recv, other, band).wait_send()
        band_copy(back_out, back_in, back_send, back_recv, other, band).wait_send()
    store.wait()


def finish_kernel(cy, ocean_ref, res_ref, smooth_ref, agg_ref, new_ref, out_ref):
    nz, cx = smooth_ref.shape[1:]
    value = smooth_ref[0]
    high = value.astype(BF16)
    low = (value - high.astype(F32)).astype(BF16)
    block = lax.broadcasted_iota(jnp.int32, (cx, cx), 0)
    for y in range(cy):
        member = jnp.where(block == agg_ref[y : y + 1, :], 1.0, 0.0).astype(BF16)
        add = jnp.dot(high, member, preferred_element_type=F32) + jnp.dot(
            low, member, preferred_element_type=F32
        )
        spot = pl.ds(y, nz, stride=cy)
        new_ref[0, spot, :] = ocean_ref[0, spot, :] + add
    out_ref[...] = res_ref[...]


def shards(
    n_band, n_tile, ocean_state, forcing, diffusivity, land_sea, aggregate, mixing, null_fields,
    coarse_op,
):
    nf, nz, cy, cx = ocean_state.shape
    cb = null_fields.shape[2]
    slab = nz // n_band
    ocean_rows = ocean_state.reshape(nf, nz * cy, cx)
    forcing_rows = forcing.reshape(nf, nz * cy, cx)
    dims = (n_band, n_tile, nf, nz, cy, cx, cb)
    any_spec = pl.BlockSpec(memory_space=pl.ANY)
    vmem = pl.BlockSpec(memory_space=pltpu.VMEM)
    smem = pl.BlockSpec(memory_space=pltpu.SMEM)
    field = pltpu.VMEM((nf, cy + 2, nz + 2 * PAD, cx), F32)
    strip = pltpu.VMEM((2, nz, cx), F32)
    slabs = pltpu.VMEM((n_band, nf // 2 * slab, 2 * cb), F32)
    dma = pltpu.SemaphoreType.DMA
    cells = nf * nz * cy * cx
    residual, smoothed = pl.pallas_call(
        functools.partial(main_kernel, dims),
        out_shape=(
            jax.ShapeDtypeStruct((nf, nz * cy, cx), F32),
            jax.ShapeDtypeStruct((nf, nz, 2 * cb), F32),
        ),
        in_specs=[any_spec, any_spec, vmem, vmem, vmem, smem, vmem, vmem],
        out_specs=(any_spec, vmem),
        scratch_shapes=[
            pltpu.VMEM((nf, nz * cy, cx), F32),
            pltpu.VMEM((nf, nz * cy, cx), F32),
            field, field, strip, strip, strip, strip,
            pltpu.VMEM((nf * nz, cx), BF16),
            pltpu.VMEM((nf * nz, cx), BF16),
            pltpu.VMEM((nf * nz, cx), F32),
            pltpu.VMEM((n_tile, 16, cx), F32),
            slabs, slabs, slabs, slabs,
            dma((nf,)), dma, dma,
            dma((2, 2)), dma((2, 2)), dma((2, 2)), dma((2, 2)),
            dma((n_tile,)), dma((n_tile,)),
            dma((n_band,)), dma((n_band,)), dma((n_band,)), dma((n_band,)),
        ],
        compiler_params=pltpu.CompilerParams(
            collective_id=0, has_side_effects=True, vmem_limit_bytes=40 * MIB
        ),
        cost_estimate=pl.CostEstimate(
            flops=60 * cells, bytes_accessed=12 * cells, transcendentals=0
        ),
    )(ocean_rows, forcing_rows, diffusivity, land_sea, aggregate, mixing, null_fields, coarse_op)

    rows_spec = pl.BlockSpec((1, nz * cy, cx), lambda f: (f, 0, 0))
    new_state, residual = pl.pallas_call(
        functools.partial(finish_kernel, cy),
        grid=(nf,),
        out_shape=(
            jax.ShapeDtypeStruct((nf, nz * cy, cx), F32),
            jax.ShapeDtypeStruct((nf, nz * cy, cx), F32),
        ),
        in_specs=[
            rows_spec, rows_spec,
            pl.BlockSpec((1, nz, 2 * cb), lambda f: (f, 0, 0)),
            pl.BlockSpec((cy, cx), lambda f: (0, 0)),
        ],
        out_specs=(rows_spec, rows_spec),
        compiler_params=pltpu.CompilerParams(vmem_limit_bytes=24 * MIB),
        cost_estimate=pl.CostEstimate(
            flops=4 * cells, bytes_accessed=16 * cells, transcendentals=0
        ),
    )(ocean_rows, residual, smoothed, aggregate)
    shape = ocean_state.shape
    return (new_state.reshape(shape), residual.reshape(shape))


def solution(mesh):
    sizes = dict(mesh.shape)
    return jax.shard_map(
        functools.partial(shards, sizes["band"], sizes["tile"]),
        mesh=mesh,
        in_specs=(
            P(None, None, "band", "tile"),
            P(None, None, "band", "tile"),
            P("band", "tile"),
            P("band", "tile"),
            P("band", "tile"),
            P(),
            P(None, None, ("band", "tile")),
            P("tile", None),
        ),
        out_specs=(P(None, None, "band", "tile"), P(None, None, "band", "tile")),
        check_vma=False,
    )
```

time: 222 us -> 58.7 us (0.26)
  local copies, waits for them, and re-layouts: 80.6 us -> 8.34 us
  matrix products: 51.1 us -> 0 us
  Pallas kernels: 0 us -> 49.3 us
  blocking collectives: 45.2 us -> 0 us
  starting transfers between devices: 32.7 us -> 0 us
  other arithmetic: 5.44 us -> 0 us
  waiting for transfers between devices: 4.29 us -> 0 us
    dot_general x9 -> x0, matrix products: 51.1 us -> none  [the longest x2 40.8 us: stencil(): jnp.einsum('fg,gzyx->fzyx', mixing, center, precision=lax.Precision.HIGHEST)]
    pallas_call x0 -> x2, Pallas kernels: none -> 49.3 us  [the longest x1 44.4 us: shards(): pl.pallas_call(functools.partial(main_kernel, dims), out_shape=(jax.Shape...]
    psum x1 -> x0, blocking collectives: 37.7 us -> none  [shards(): gram, proj = lax.psum((gram_part, proj_part), 'tile')]
    slice x9 -> x0, local copies, waits for them, and re-layouts: 25.3 us -> none  [the longest x4 17.5 us: padded_2(): lax.slice_in_dim(block, block.shape[dim] - width, None, axis=dim)]
    ppermute x8 -> x0, starting transfers between devices: 24.8 us -> none  [the longest x4 19.4 us: padded_2(): lax.ppermute(lax.slice_in_dim(block, block.shape[dim] - width, None, axis...]
    ppermute x4 -> x0, local copies, waits for them, and re-layouts: 14.1 us -> none  [the longest x2 7.43 us: padded_2(): lax.ppermute(lax.slice_in_dim(block, block.shape[dim] - width, None, axis...]
    unnamed x40 -> x16, local copies, waits for them, and re-layouts: 19.7 us -> 8.34 us
    all_to_all x1 -> x0, starting transfers between devices: 7.96 us -> none  [shards(): lax.all_to_all(deflated, 'band', split_axis=1, concat_axis=2, tiled=True)]
  transfers between devices with their start and end apart: 9 -> 0, of which waited for: 3 -> 0; matrix products, arithmetic and copies ran while one was open for 9% -> 0% of each run, Pallas kernels for 0% -> 0%
where the time goes in v1:
time: 58.7 us; the launch traced here: 58.2 us
  Pallas kernels  49.3 us (84%)
  local copies, waits for them, and re-layouts  8.34 us (14%)
  between operations  0.66 us (1%)
    pallas_call x1, Pallas kernels, shards(): pl.pallas_call(functools.partial(main_kernel, dims), out_shape=(jax.Shape...  44.4 us
    unnamed x16, local copies, waits for them, and re-layouts  8.34 us
    pallas_call x1, Pallas kernels, shards(): pl.pallas_call(functools.partial(finish_kernel, cy), grid=(nf,), out_shap...  4.83 us

profile of v1, /device:TPU:0, one launch (start us, length us, event | category | flops | bytes accessed | tf_op | source)
XLA Modules:
  0.0 58.2 jit_solution(6429911738747171171)
XLA Ops:
  0.6 0.0 copy-start
  0.6 1.9 %copy-done = f32[6,64,16,128]{3,2,1,0:T(8,128)S(1)} copy-done((f32[6,64,16,128]{3,2,1,0:T(8,128)S(1)}, f32[6,64,16,128]{3,2,1,0:T(8,128)}, u32[]{:S(2)}) %copy-start) | copy-done | bytes 3145752
  2.5 0.0 copy-start.1
  2.5 1.9 %copy-done.1 = f32[6,64,16,128]{3,2,1,0:T(8,128)S(1)} copy-done((f32[6,64,16,128]{3,2,1,0:T(8,128)S(1)}, f32[6,64,16,128]{3,2,1,0:T(8,128)}, u32[]{:S(2)}) %copy-start.1) | copy-done | bytes 3145752
  4.4 0.0 copy-start.2
  4.4 0.9 %copy-done.2 = f32[256,256]{1,0:T(8,128)S(1)} copy-done((f32[256,256]{1,0:T(8,128)S(1)}, f32[256,256]{1,0:T(8,128)}, u32[]{:S(2)}) %copy-start.2) | copy-done | bytes 262168
  5.4 0.0 copy-start.3
  5.4 0.8 %copy-done.3 = f32[2,64,64]{2,1,0:T(8,128)S(1)} copy-done((f32[2,64,64]{2,1,0:T(8,128)S(1)}, f32[2,64,64]{2,1,0:T(8,128)}, u32[]{:S(2)}) %copy-start.3) | copy-done | bytes 32792
  6.2 0.0 copy-start.4
  6.2 0.7 %copy-done.4 = s32[16,128]{1,0:T(8,128)S(1)} copy-done((s32[16,128]{1,0:T(8,128)S(1)}, s32[16,128]{1,0:T(8,128)}, u32[]{:S(2)}) %copy-start.4) | copy-done | bytes 8216
  6.9 0.0 copy-start.5
  6.9 0.7 %copy-done.5 = f32[16,128]{1,0:T(8,128)S(1)} copy-done((f32[16,128]{1,0:T(8,128)S(1)}, f32[16,128]{1,0:T(8,128)}, u32[]{:S(2)}) %copy-start.5) | copy-done | bytes 8216
  7.6 0.0 copy-start.6
  7.6 0.7 %copy-done.6 = s32[16,128]{1,0:T(8,128)S(1)} copy-done((s32[16,128]{1,0:T(8,128)S(1)}, s32[16,128]{1,0:T(8,128)}, u32[]{:S(2)}) %copy-start.6) | copy-done | bytes 8216
  8.3 0.0 copy-start.7
  8.3 0.7 %copy-done.7 = f32[6,6]{1,0:T(8,128)S(1)} copy-done((f32[6,6]{1,0:T(8,128)S(1)}, f32[6,6]{1,0:T(8,128)}, u32[]{:S(2)}) %copy-start.7) | copy-done | bytes 168
  9.0 44.4 %shard_map.95 = (f32[6,1024,128]{2,1,0:T(8,128)S(1)}, f32[6,64,128]{2,1,0:T(8,128)S(1)}) custom-call(f32[6,1024,128]{2,1,0:T(8,128)S(1)} %bitcast.4, f32[6,1024,128]{2,1,0:T(8,128)S(1)} %bitcast.6, f32[16,128]{1,0:T(8,128)S(1)} %copy-done.5, s32[16,128]{1,0:T(8,128)S(1)} %copy-done.6, s32[16,128]{1,0:T(8,128)S(1)} %copy-done.4, f32[6,6]{1,0:T(8,128)S(1)} %copy-done.7, ...), custom_call_target="tpu_custom_call" | custom-call | flops 47185920 | bytes 9437184 | tf_op jit(solution)/shard_map/pallas_call | solution.py:377
  53.4 4.8 %shard_map.96 = (f32[6,1024,128]{2,1,0:T(8,128)}, f32[6,1024,128]{2,1,0:T(8,128)}) custom-call(f32[6,1024,128]{2,1,0:T(8,128)S(1)} %bitcast.5, f32[6,1024,128]{2,1,0:T(8,128)S(1)} %get-tuple-element.6.res_ref, f32[6,64,128]{2,1,0:T(8,128)S(1)} %get-tuple-element.7.smooth_ref, s32[16,128]{1,0:T(8,128)S(1)} %copy-done.4), custom_call_target="tpu_custom_call" | custom-call | flops 3145728 | bytes 12582912 | tf_op jit(solution)/shard_map/pallas_call | solution.py:408
Async XLA Ops:
  0.6 1.9 %copy-start = (f32[6,64,16,128]{3,2,1,0:T(8,128)S(1)}, f32[6,64,16,128]{3,2,1,0:T(8,128)}, u32[]{:S(2)}) copy-start(f32[6,64,16,128]{3,2,1,0:T(8,128)} %param.8) | copy-start | bytes 9437188
  2.5 1.9 %copy-start.1 = (f32[6,64,16,128]{3,2,1,0:T(8,128)S(1)}, f32[6,64,16,128]{3,2,1,0:T(8,128)}, u32[]{:S(2)}) copy-start(f32[6,64,16,128]{3,2,1,0:T(8,128)} %param.9) | copy-start | bytes 9437188
  4.4 0.9 %copy-start.2 = (f32[256,256]{1,0:T(8,128)S(1)}, f32[256,256]{1,0:T(8,128)}, u32[]{:S(2)}) copy-start(f32[256,256]{1,0:T(8,128)} %op_ref.1) | copy-start | bytes 786436
  5.4 0.8 %copy-start.3 = (f32[2,64,64]{2,1,0:T(8,128)S(1)}, f32[2,64,64]{2,1,0:T(8,128)}, u32[]{:S(2)}) copy-start(f32[2,64,64]{2,1,0:T(8,128)} %null_ref.1) | copy-start | bytes 98308
  6.2 0.7 %copy-start.4 = (s32[16,128]{1,0:T(8,128)S(1)}, s32[16,128]{1,0:T(8,128)}, u32[]{:S(2)}) copy-start(s32[16,128]{1,0:T(8,128)} %agg_ref.3) | copy-start | bytes 24580
  6.9 0.7 %copy-start.5 = (f32[16,128]{1,0:T(8,128)S(1)}, f32[16,128]{1,0:T(8,128)}, u32[]{:S(2)}) copy-start(f32[16,128]{1,0:T(8,128)} %diff_ref.1) | copy-start | bytes 24580
  7.6 0.7 %copy-start.6 = (s32[16,128]{1,0:T(8,128)S(1)}, s32[16,128]{1,0:T(8,128)}, u32[]{:S(2)}) copy-start(s32[16,128]{1,0:T(8,128)} %land_ref.1) | copy-start | bytes 24580
  8.3 0.7 %copy-start.7 = (f32[6,6]{1,0:T(8,128)S(1)}, f32[6,6]{1,0:T(8,128)}, u32[]{:S(2)}) copy-start(f32[6,6]{1,0:T(8,128)} %mix_ref.1) | copy-start | bytes 436

commit v2 on v1

--- a/solution.py
+++ b/solution.py
@@ -17,7 +17,7 @@
 BF16 = jnp.bfloat16
 MESH = pl.DeviceIdType.MESH
 PAD = 8
-ZC = 16
+ZC = 64
 MIB = 1 << 20
 
 
@@ -28,9 +28,10 @@
 
 
 def main_kernel(
-    dims, ocean_ref, forcing_ref, diff_ref, land_ref, agg_ref, mix_ref, null_ref, op_ref,
+    dims, ocean_ref, forcing_ref, diff_hbm, land_hbm, agg_hbm, mix_hbm, null_hbm, op_hbm,
     res_ref, smooth_ref,
-    ocean, work, field0, field1, send_w, send_e, col_w, col_e, hi, lo, coarse,
+    diff_ref, land_ref, agg_ref, mix_ref, null_ref, op_ref, small_sem,
+    ocean, work, field0, field1, edges, halo, col_w, col_e, hi, lo, coarse,
     mom, slab_out, slab_in, back_out, back_in,
     in_sem, work_sem, out_sem, lat_send, lat_recv, lon_send, lon_recv,
     mom_send, mom_recv, slab_send, slab_recv, back_send, back_recv,
@@ -44,6 +45,17 @@
     ]
     for load in loads:
         load.start()
+    smalls = [
+        pltpu.make_async_copy(source, target, small_sem.at[i])
+        for i, (source, target) in enumerate(
+            (
+                (diff_hbm, diff_ref), (land_hbm, land_ref), (agg_hbm, agg_ref),
+                (mix_hbm, mix_ref), (null_hbm, null_ref), (op_hbm, op_ref),
+            )
+        )
+    ]
+    for load in smalls:
+        load.start()
     load_forcing = pltpu.make_async_copy(forcing_ref, work, work_sem)
     load_forcing.start()
 
@@ -73,7 +85,7 @@
         for field in (field0, field1):
             field[:, cy + 1, PAD:top, :] = zrow
 
-    zcol = jnp.zeros((2, nz, cx), F32)
+    zcol = jnp.zeros((2, 2, nz, cx), F32)
 
     @pl.when(tile == 0)
     def _():
@@ -83,33 +95,37 @@
     def _():
         col_e[...] = zcol
 
-    send_w[...] = zcol
-    send_e[...] = zcol
+    edges[...] = zcol
     coarse[...] = jnp.zeros_like(coarse)
 
     lane = lax.broadcasted_iota(jnp.int32, (ZC, cx), 1)
 
-    def pack(which, value, rows, k):
-        here = lane == k
-        send_w[which, rows, :] = jnp.where(here, pltpu.roll(value, k, 1), send_w[which, rows, :])
-        shift = lax.rem(k + 1, cx)
-        send_e[which, rows, :] = jnp.where(
-            here, pltpu.roll(value, shift, 1), send_e[which, rows, :]
-        )
+    pair = lane // 2
+    group_rows = cy // 2
+
+    def place(f, y):
+        return f * group_rows + lax.rem(y + cy - 1, group_rows)
+
+    def pack(carry, value, k):
+        return jnp.where(pair == k, pltpu.roll(value, 2 * k + 1, 1), carry)
+
+    def sweep(body, which, group, start, stop, stride=1):
+        for z0 in range(0, nz, ZC):
+            packed = lax.fori_loop(
+                start, stop, lambda i, carry: body(z0, i * stride, carry), jnp.zeros((ZC, cx), F32)
+            )
+            rows = slice(z0, z0 + ZC)
+            edges[which, group, rows, :] = edges[which, group, rows, :] + packed
 
     for f in range(nf):
         loads[f].wait()
 
-    def fill(y, carry):
+    def fill(z0, y, carry):
         for f in range(nf):
-            for z0 in range(0, nz, ZC):
-                value = ocean[f, pl.ds(z0 * cy + y, ZC, stride=cy), :]
-                field0[f, y + 1, PAD + z0 : PAD + z0 + ZC, :] = value
-                pack(0, value, slice(z0, z0 + ZC), f * cy + y)
+            value = ocean[f, pl.ds(z0 * cy + y, ZC, stride=cy), :]
+            field0[f, y + 1, PAD + z0 : PAD + z0 + ZC, :] = value
+            carry = pack(carry, value, place(f, y))
         return carry
-
-    lax.fori_loop(0, cy, fill, 0)
-    pl.semaphore_wait(barrier, n_tile + n_band - 2)
 
     def lat_copies(which, field):
         up = pltpu.make_async_remote_copy(
@@ -124,15 +140,15 @@
         )
         return up, down
 
-    def lon_copies(which):
+    def lon_copies(which, group):
         up = pltpu.make_async_remote_copy(
-            src_ref=send_e.at[which], dst_ref=col_w.at[which],
-            send_sem=lon_send.at[which, 0], recv_sem=lon_recv.at[which, 0],
+            src_ref=edges.at[which, group], dst_ref=col_w.at[which, group],
+            send_sem=lon_send.at[which, group, 0], recv_sem=lon_recv.at[which, group, 0],
             device_id=(band, tile + 1), device_id_type=MESH,
         )
         down = pltpu.make_async_remote_copy(
-            src_ref=send_w.at[which], dst_ref=col_e.at[which],
-            send_sem=lon_send.at[which, 1], recv_sem=lon_recv.at[which, 1],
+            src_ref=edges.at[which, group], dst_ref=col_e.at[which, group],
+            send_sem=lon_send.at[which, group, 1], recv_sem=lon_recv.at[which, group, 1],
             device_id=(band, tile - 1), device_id_type=MESH,
         )
         return up, down
@@ -155,6 +171,14 @@
         def _():
             copies[1].wait_recv()
 
+    even = lax.broadcasted_iota(jnp.int32, (nz, cx), 1) % 2 == 0
+
+    def recv_lon(which, group):
+        recv_both(lon[which][group], tile, n_tile)
+        halo[which, group] = jnp.where(
+            even, col_w[which, group], pltpu.roll(col_e[which, group], cx - 2, 1)
+        )
+
     def sent_both(copies, index, count):
         @pl.when(index < count - 1)
         def _():
@@ -164,29 +188,21 @@
         def _():
             copies[1].wait_send()
 
-    def exchange(which, field):
-        lon, lat = lon_copies(which), lat_copies(which, field)
-        start_both(lon, tile, n_tile)
-        start_both(lat, band, n_band)
-        return lon, lat
-
-    def jacobian_rows(which, field, y, z0):
+    def jacobian_rows(which, group, field, y, z0):
         at = PAD + z0
         rows = slice(at, at + ZC)
         center = [field[g, y + 1, rows, :] for g in range(nf)]
         diff = diff_ref[pl.ds(y, 1), :]
         main = 4.0 * diff + (1.0 + 2.0 * VERTICAL_MIX)
         ocean_cell = jnp.broadcast_to(land_ref[pl.ds(y, 1), :], (ZC, cx)) != 0
-        west_in = col_w[which, z0 : z0 + ZC, :]
-        east_in = col_e[which, z0 : z0 + ZC, :]
+        beside = halo[which, group, z0 : z0 + ZC, :]
         outs = []
         for f in range(nf):
             c = center[f]
-            k = f * cy + y
-            west = jnp.where(lane == 0, pltpu.roll(west_in, cx - k, 1), pltpu.roll(c, 1, 1))
-            east = jnp.where(
-                lane == cx - 1, pltpu.roll(east_in, cx - 1 - k, 1), pltpu.roll(c, cx - 1, 1)
-            )
+            k = place(f, y)
+            outer = pltpu.roll(beside, lax.rem(cx - 2 * k, cx), 1)
+            west = jnp.where(lane == 0, outer, pltpu.roll(c, 1, 1))
+            east = jnp.where(lane == cx - 1, outer, pltpu.roll(c, cx - 1, 1))
             around = field[f, y, rows, :] + field[f, y + 2, rows, :] + (east + west)
             vert = field[f, y + 1, at - 1 : at - 1 + ZC, :] + field[f, y + 1, at + 1 : at + 1 + ZC, :]
             total = main * c - diff * around - VERTICAL_MIX * vert + SPEED_TABLE[f] * (east - west)
@@ -195,17 +211,19 @@
             outs.append(jnp.where(ocean_cell, total, c))
         return center, outs
 
-    def first(y, carry):
-        for z0 in range(0, nz, ZC):
-            center, outs = jacobian_rows(0, field0, y, z0)
+    def first(group):
+        def body(z0, y, carry):
+            center, outs = jacobian_rows(0, group, field0, y, z0)
             for f in range(nf):
                 field1[f, y + 1, PAD + z0 : PAD + z0 + ZC, :] = outs[f]
-                pack(1, outs[f], slice(z0, z0 + ZC), f * cy + y)
-        return carry
-
-    def second(y, carry):
+                carry = pack(carry, outs[f], place(f, y))
+            return carry
+
+        return body
+
+    def second(group, y, carry):
         for z0 in range(0, nz, ZC):
-            center, outs = jacobian_rows(1, field1, y, z0)
+            center, outs = jacobian_rows(1, group, field1, y, z0)
             for f in range(nf):
                 spot = pl.ds(z0 * cy + y, ZC, stride=cy)
                 value = work[f, spot, :] - (center[f] + TIME_WEIGHT * outs[f])
@@ -218,19 +236,37 @@
         coarse[...] += nt_dot(hi[...], member) + nt_dot(lo[...], member)
         return carry
 
-    ends = lambda body: lax.fori_loop(0, 2, lambda i, carry: body(i * (cy - 1), carry), 0)
-
-    lon0, lat0 = exchange(0, field0)
-    recv_both(lon0, tile, n_tile)
-    lax.fori_loop(1, cy - 1, first, 0)
-    recv_both(lat0, band, n_band)
-    ends(first)
-    lon1, lat1 = exchange(1, field1)
+    mid, last = cy // 2 + 1, cy - 1
+    lon = [[lon_copies(which, group) for group in range(2)] for which in range(2)]
+    lat = [lat_copies(0, field0), lat_copies(1, field1)]
+
+    sweep(fill, 0, 0, 1, mid)
+    pl.semaphore_wait(barrier, n_tile + n_band - 2)
+    start_both(lon[0][0], tile, n_tile)
+    sweep(fill, 0, 1, 0, 2, last)
+    start_both(lat[0], band, n_band)
+    sweep(fill, 0, 1, mid, last)
+    start_both(lon[0][1], tile, n_tile)
+    for load in smalls:
+        load.wait()
+
+    recv_lon(0, 0)
+    sweep(first(0), 1, 0, 1, mid)
+    start_both(lon[1][0], tile, n_tile)
+    recv_lon(0, 1)
+    recv_both(lat[0], band, n_band)
+    sweep(first(1), 1, 1, 0, 2, last)
+    start_both(lat[1], band, n_band)
+    sweep(first(1), 1, 1, mid, last)
+    start_both(lon[1][1], tile, n_tile)
+
     load_forcing.wait()
-    recv_both(lon1, tile, n_tile)
-    lax.fori_loop(1, cy - 1, second, 0)
-    recv_both(lat1, band, n_band)
-    ends(second)
+    recv_lon(1, 0)
+    lax.fori_loop(1, mid, functools.partial(second, 0), 0)
+    recv_lon(1, 1)
+    lax.fori_loop(mid, last, functools.partial(second, 1), 0)
+    recv_both(lat[1], band, n_band)
+    lax.fori_loop(0, 2, lambda i, carry: second(1, i * last, carry), 0)
     store = pltpu.make_async_copy(work, res_ref, out_sem)
     store.start()
 
@@ -328,9 +364,10 @@
             smooth_ref[f, z, :] = jnp.where(inside, both, 0.0)
             smooth_ref[f + half, z, :] = jnp.where(inside, pltpu.roll(both, cb, 1), 0.0)
 
-    for lon, lat in ((lon0, lat0), (lon1, lat1)):
-        sent_both(lon, tile, n_tile)
-        sent_both(lat, band, n_band)
+    for which in range(2):
+        sent_both(lat[which], band, n_band)
+        for group in range(2):
+            sent_both(lon[which][group], tile, n_tile)
     for d in range(1, n_tile):
         mom_copy(lax.rem(tile + d, n_tile), tile).wait_send()
     for d in range(1, n_band):
@@ -368,9 +405,8 @@
     dims = (n_band, n_tile, nf, nz, cy, cx, cb)
     any_spec = pl.BlockSpec(memory_space=pl.ANY)
     vmem = pl.BlockSpec(memory_space=pltpu.VMEM)
-    smem = pl.BlockSpec(memory_space=pltpu.SMEM)
     field = pltpu.VMEM((nf, cy + 2, nz + 2 * PAD, cx), F32)
-    strip = pltpu.VMEM((2, nz, cx), F32)
+    strip = pltpu.VMEM((2, 2, nz, cx), F32)
     slabs = pltpu.VMEM((n_band, nf // 2 * slab, 2 * cb), F32)
     dma = pltpu.SemaphoreType.DMA
     cells = nf * nz * cy * cx
@@ -380,9 +416,16 @@
             jax.ShapeDtypeStruct((nf, nz * cy, cx), F32),
             jax.ShapeDtypeStruct((nf, nz, 2 * cb), F32),
         ),
-        in_specs=[any_spec, any_spec, vmem, vmem, vmem, smem, vmem, vmem],
+        in_specs=[any_spec] * 8,
         out_specs=(any_spec, vmem),
         scratch_shapes=[
+            pltpu.VMEM(diffusivity.shape, F32),
+            pltpu.VMEM(land_sea.shape, land_sea.dtype),
+            pltpu.VMEM(aggregate.shape, aggregate.dtype),
+            pltpu.SMEM(mixing.shape, F32),
+            pltpu.VMEM(null_fields.shape, F32),
+            pltpu.VMEM(coarse_op.shape, F32),
+            dma((6,)),
             pltpu.VMEM((nf, nz * cy, cx), F32),
             pltpu.VMEM((nf, nz * cy, cx), F32),
             field, field, strip, strip, strip, strip,
@@ -392,12 +435,12 @@
             pltpu.VMEM((n_tile, 16, cx), F32),
             slabs, slabs, slabs, slabs,
             dma((nf,)), dma, dma,
-            dma((2, 2)), dma((2, 2)), dma((2, 2)), dma((2, 2)),
+            dma((2, 2)), dma((2, 2)), dma((2, 2, 2)), dma((2, 2, 2)),
             dma((n_tile,)), dma((n_tile,)),
             dma((n_band,)), dma((n_band,)), dma((n_band,)), dma((n_band,)),
         ],
         compiler_params=pltpu.CompilerParams(
-            collective_id=0, has_side_effects=True, vmem_limit_bytes=40 * MIB
+            collective_id=0, has_side_effects=True, vmem_limit_bytes=60 * MIB
         ),
         cost_estimate=pl.CostEstimate(
             flops=60 * cells, bytes_accessed=12 * cells, transcendentals=0

time: 58.7 us -> 47 us (0.80)
  Pallas kernels: 49.3 us -> 43.3 us
  local copies, waits for them, and re-layouts: 8.34 us -> 2.82 us
    pallas_call x1, Pallas kernels: 44.4 us -> 38.5 us  [shards(): pl.pallas_call(functools.partial(main_kernel, dims), out_shape=(jax.Shape...]
    unnamed x16 -> x8, local copies, waits for them, and re-layouts: 8.34 us -> 2.82 us
where the time goes in v2:
time: 47 us; the launch traced here: 46.8 us
  Pallas kernels  43.3 us (92%)
  local copies, waits for them, and re-layouts  2.82 us (6%)
  between operations  0.68 us (1%)
    pallas_call x1, Pallas kernels, shards(): pl.pallas_call(functools.partial(main_kernel, dims), out_shape=(jax.Shape...  38.5 us
    pallas_call x1, Pallas kernels, shards(): pl.pallas_call(functools.partial(finish_kernel, cy), grid=(nf,), out_shap...  4.75 us
    unnamed x8, local copies, waits for them, and re-layouts  2.82 us

profile of v2, /device:TPU:0, one launch (start us, length us, event | category | flops | bytes accessed | tf_op | source)
XLA Modules:
  0.0 46.8 jit_solution(14954492103502184158)
XLA Ops:
  0.6 0.0 copy-start
  0.6 0.0 copy-start.3
  0.7 38.5 %shard_map.95 = (f32[6,1024,128]{2,1,0:T(8,128)}, f32[6,64,128]{2,1,0:T(8,128)}) custom-call(f32[6,1024,128]{2,1,0:T(8,128)} %bitcast.4, f32[6,1024,128]{2,1,0:T(8,128)} %bitcast.6, f32[16,128]{1,0:T(8,128)} %diff_hbm.1, s32[16,128]{1,0:T(8,128)} %land_hbm.1, s32[16,128]{1,0:T(8,128)} %agg_ref.1, f32[6,6]{1,0:T(8,128)} %mix_hbm.1, f32[2,64,64]{2,1,0:T(8,128)} %null_hbm.1, ...), custom_call_target="tpu_custom_call" | custom-call | flops 47185920 | bytes 9437184 | tf_op jit(solution)/shard_map/pallas_call | solution.py:413
  39.2 0.0 copy-done
  39.2 0.0 copy-done.3
  39.2 0.0 copy-start.1
  39.2 1.9 %copy-done.1 = f32[6,1024,128]{2,1,0:T(8,128)S(1)} copy-done((f32[6,1024,128]{2,1,0:T(8,128)S(1)}, f32[6,1024,128]{2,1,0:T(8,128)}, u32[]{:S(2)}) %copy-start.1) | copy-done | bytes 3145752
  41.1 0.0 copy-start.2
  41.1 0.9 %copy-done.2 = f32[6,64,128]{2,1,0:T(8,128)S(1)} copy-done((f32[6,64,128]{2,1,0:T(8,128)S(1)}, f32[6,64,128]{2,1,0:T(8,128)}, u32[]{:S(2)}) %copy-start.2) | copy-done | bytes 196632
  42.0 4.8 %shard_map.96 = (f32[6,1024,128]{2,1,0:T(8,128)}, f32[6,1024,128]{2,1,0:T(8,128)}) custom-call(f32[6,1024,128]{2,1,0:T(8,128)S(1)} %bitcast.5, f32[6,1024,128]{2,1,0:T(8,128)S(1)} %copy-done.1, f32[6,64,128]{2,1,0:T(8,128)S(1)} %copy-done.2, s32[16,128]{1,0:T(8,128)S(1)} %copy-done.3), custom_call_target="tpu_custom_call" | custom-call | flops 3145728 | bytes 12582912 | tf_op jit(solution)/shard_map/pallas_call | solution.py:451
Async XLA Ops:
  0.6 38.6 %copy-start = (f32[6,64,16,128]{3,2,1,0:T(8,128)S(1)}, f32[6,64,16,128]{3,2,1,0:T(8,128)}, u32[]{:S(2)}) copy-start(f32[6,64,16,128]{3,2,1,0:T(8,128)} %param.8) | copy-start | bytes 9437188
  0.6 38.6 %copy-start.3 = (s32[16,128]{1,0:T(8,128)S(1)}, s32[16,128]{1,0:T(8,128)}, u32[]{:S(2)}) copy-start(s32[16,128]{1,0:T(8,128)} %agg_ref.1) | copy-start | bytes 24580
  39.2 1.9 %copy-start.1 = (f32[6,1024,128]{2,1,0:T(8,128)S(1)}, f32[6,1024,128]{2,1,0:T(8,128)}, u32[]{:S(2)}) copy-start(f32[6,1024,128]{2,1,0:T(8,128)} %get-tuple-element.6.res_ref) | copy-start | bytes 9437188
  41.1 0.9 %copy-start.2 = (f32[6,64,128]{2,1,0:T(8,128)S(1)}, f32[6,64,128]{2,1,0:T(8,128)}, u32[]{:S(2)}) copy-start(f32[6,64,128]{2,1,0:T(8,128)} %get-tuple-element.7.smooth_ref) | copy-start | bytes 589828
